TPU v7x, 256 devices: a whole 4x4x8 slice. The times are simulated.
256 devices in a mesh: grp: 8 (over x, core), tp: 32 (over y, z).
Axes of the slice: x: 4, y: 4, z: 8, core: 2. Of those that a mesh axis runs over, the one named last changes fastest.
Arguments:
- queries: bfloat16 [256, 8192], P('grp', 'tp'), may hold values from -12 to 12
- prefix_ids: int32 [256, 1], P('grp'), may hold values from 0 to 15; in each aligned block of 32 rows (0 to 31, 32 to 63, ...) at most 4 rows name the same one
- suffix_lengths: int32 [256], P('grp'), may hold values from 2 to 512
- owner_slots: int32 [16], replicated, may hold values from 0 to 15, each once
- prefix_cache: bfloat16 [2, 16, 8192, 1024], P(None, 'grp', 'tp'), may hold values from -5 to 5
- suffix_cache: bfloat16 [2, 256, 512, 1024], P(None, 'grp', 'tp'), may hold values from -5 to 5
- wo: bfloat16 [8192, 8192], P('tp'), may hold values from -0.0625 to 0.0625
Outputs:
- layer_out: bfloat16 [256, 8192], P('grp', 'tp')
Inputs may be any that keep to these rules, and one draw needn't show every extreme that they name: `prefix_ids`: in the rows of one index of grp (aligned blocks of 32 requests) no prefix id appears more than 4 times. `owner_slots`: A permutation; slot j of prefix_cache lies on index j // 2 of grp.
All inputs are finite; a program needn't handle non-finite values.
Results may differ from a plain program's by a relative error of at most 0.024.
Values may be sent and summed in bfloat16 or wider, within the bound.
A program may use at most 128 MiB of HBM per device.

v0:
```python
import functools
import math

import jax
import jax.numpy as jnp
from jax import lax
from jax.experimental import pallas as pl
from jax.experimental.pallas import tpu as pltpu
from jax.sharding import PartitionSpec as P

HD = 128
OWN = 2
SLOTS = 2
CAP = 4
LANES = SLOTS * CAP
Z_SIZE = 8
NEAR = 6
MASKED = -1e30
MESH = pl.DeviceIdType.MESH


def div(a, b):
    return a // b if isinstance(a, int) else lax.div(a, jnp.full_like(a, b))


def rem(a, b):
    return a % b if isinstance(a, int) else lax.rem(a, jnp.full_like(a, b))


def turn(i):
    return i + div(i, 2) * (1 - 2 * rem(i, 2))


def outward(i, count):
    return count // 2 + (1 - 2 * rem(i, 2)) * div(i + 1, 2)


def nt(a, b):
    return lax.dot_general(a, b, (((1,), (1,)), ((), ())), preferred_element_type=jnp.float32)


def mm(a, b):
    return jnp.dot(a, b, preferred_element_type=jnp.float32)


def iota(shape, dim):
    return lax.broadcasted_iota(jnp.int32, shape, dim)


def diagonal(rows, shift=0):
    return iota((rows, 128), 1) == iota((rows, 128), 0) + shift


def to_row(column, rows):
    wide = jnp.broadcast_to(column, (rows, 128))
    return jnp.sum(jnp.where(diagonal(rows), wide, 0.0), axis=0, keepdims=True)


def to_column(row, rows, shift=0):
    wide = jnp.broadcast_to(row, (rows, 128))
    return jnp.sum(jnp.where(diagonal(rows, shift), wide, 0.0), axis=1, keepdims=True)


def merge(parts):
    largest = functools.reduce(jnp.maximum, [level for _, level in parts])
    factors = [jnp.exp(level - largest) for _, level in parts]
    total = functools.reduce(jnp.add, factors)
    summed = functools.reduce(jnp.add, [f * value for f, (value, _) in zip(factors, parts)])
    return summed / total, largest + jnp.log(total)


def spread(row, shape, index):
    return jnp.sum(jnp.where(iota(shape, 1) == index, row, 0.0), axis=1, keepdims=True)


def attend(products, values):
    scale = 1.0 / math.sqrt(HD)
    highest = jnp.max(products, axis=1, keepdims=True)
    weights = jnp.exp((products - highest) * scale)
    totals = jnp.sum(weights, axis=1, keepdims=True)
    summed = mm(weights.astype(jnp.bfloat16), values)
    return summed / totals, highest * scale + jnp.log(totals)


def kernel(
    dims,
    q_ref, ids_ref, len_ref, slots_ref, pc_ref, sc_ref, wo_ref, out_ref,
    qv, idv, lenv, slotv, pk, sk, wv, qall, xs, xr, po, pr, ls, lr, fr, flr, fo, fl, lc, so, sl, sel, back, gsel, lsel, bias,
    yb, yl, yr, ylr, ur, ulr, vb, vl, vr, vlr, zb, zl, zr, zlr, wp, wr, wz, wzr, wur, wvb, wvr,
    in_sem, a_send, a_recv, b_send, b_recv, o_send, o_recv, w_send, w_recv, c_send, c_recv, f_send, f_recv,
    e_send, e_recv, el_send, el_recv, r_send, r_recv, rl_send, rl_recv, m_send, m_recv, ml_send, ml_recv,
    y_send, y_recv, yl_send, yl_recv, z_send, z_recv, zl_send, zl_recv,
    u_send, u_recv, ul_send, ul_recv, v_send, v_recv, wu_send, wu_recv, wv_send, wv_recv,
    wy_send, wy_recv, wz_send, wz_recv,
):
    groups, ys, zs, kvh, rows, suf = dims
    ky = kvh // ys
    dk = ys * zs // kvh
    size = dk * OWN
    n = size * rows
    strip = SLOTS * size * CAP
    lane_rows = ky * strip
    small = size * CAP
    half = rows // 2
    grp = lax.axis_index("grp")
    tp = lax.axis_index("tp")
    y = div(tp, zs)
    z = rem(tp, zs)

    opposite = ys // 2
    beside = [d for d in range(1, ys) if d != opposite]

    def remote(src, dst, send, recv, device):
        return pltpu.make_async_remote_copy(
            src_ref=src, dst_ref=dst, send_sem=send, recv_sem=recv,
            device_id=device, device_id_type=MESH,
        )

    def each(low, high, fn):
        def step(i, c):
            fn(i)
            return c
        lax.fori_loop(low, high, step, 0)

    loads = [
        pltpu.make_async_copy(q_ref, qv, in_sem.at[0]),
        pltpu.make_async_copy(ids_ref, idv, in_sem.at[1]),
        pltpu.make_async_copy(len_ref, lenv, in_sem.at[2]),
        pltpu.make_async_copy(slots_ref, slotv, in_sem.at[3]),
        pltpu.make_async_copy(sc_ref, sk, in_sem.at[4]),
        pltpu.make_async_copy(pc_ref, pk, in_sem.at[5]),
        pltpu.make_async_copy(wo_ref, wv, in_sem.at[6]),
    ]
    for load in loads:
        load.start()

    def z_peer(d):
        return (grp, y * zs + rem(z + d, zs))

    def y_peer(d):
        return (grp, rem(y + d, ys) * zs + z)

    def y_back(d):
        return (grp, rem(y - d + ys, ys) * zs + z)

    def owner(e):
        x, core = rem(div(grp, 2) + turn(div(e, 2)), groups // 2), rem(grp + e, 2)
        return x * 2 + core

    def asker(e):
        x, core = rem(div(grp, 2) + groups // 2 - turn(div(e, 2)), groups // 2), rem(grp + e, 2)
        return x * 2 + core

    barrier = pltpu.get_barrier_semaphore()
    each(1, zs, lambda d: pl.semaphore_signal(barrier, inc=1, device_id=z_peer(d), device_id_type=MESH))
    each(1, ys, lambda d: pl.semaphore_signal(barrier, inc=1, device_id=y_peer(d), device_id_type=MESH))
    each(1, groups, lambda d: pl.semaphore_signal(barrier, inc=1, device_id=(owner(d), tp), device_id_type=MESH))

    loads[0].wait()
    qall[tp, 0:rows, :] = qv[:, 0:HD]
    qall[tp, rows : 2 * rows, :] = qv[:, HD : 2 * HD]
    pl.semaphore_wait(barrier, zs + ys + groups - 3)

    def a_copy(d):
        return remote(qall.at[tp], qall.at[tp], a_send.at[d], a_recv.at[d], z_peer(d))

    def b_copy(d):
        row = qall.at[pl.ds(y * zs, zs)]
        return remote(row, row, b_send.at[d], b_recv.at[d], y_peer(d))

    def o_copy():
        return remote(qall.at[tp], qall.at[tp], o_send.at[0], o_recv.at[0], y_peer(opposite))

    def w_copy(d):
        piece = qall.at[rem(y + opposite, ys) * zs + z]
        return remote(piece, piece, w_send.at[d], w_recv.at[d], z_peer(d))

    each(0, zs - 1, lambda i: a_copy(outward(i, zs)).start())
    o_copy().start()

    for load in loads[1:4]:
        load.wait()
    ids = idv[...].astype(jnp.float32)
    lengths = lenv[...].astype(jnp.float32)
    slot_count = slotv.shape[1]
    slots = spread(slotv[...].astype(jnp.float32), (slot_count,) * 2, iota((slot_count,) * 2, 0))
    square = (rows, rows)
    ids_column = spread(ids, square, iota(square, 0))
    slot_of = jnp.sum(
        jnp.where(iota((slot_count, rows), 0).astype(jnp.float32) == ids, slots, 0.0),
        axis=0, keepdims=True,
    )
    earlier = (ids_column == ids) & (iota(square, 0) < iota(square, 1))
    target = slot_of * CAP + jnp.sum(jnp.where(earlier, 1.0, 0.0), axis=0, keepdims=True)
    target_column = spread(target, square, iota(square, 0))
    all_rows = jnp.sum(
        jnp.where(iota((rows, n), 0) == rem(iota((rows, n), 1), rows), target_column, 0.0),
        axis=0, keepdims=True,
    ).astype(jnp.int32) + (groups * LANES) * (div(iota((1, n), 1), rows))
    all_column = spread(target, (n, rows), rem(iota((n, rows), 0), rows)).astype(jnp.int32)
    head = div(iota((n, 128), 0), rows)
    place = jnp.broadcast_to(all_column, (n, 128))
    gsel[...] = div(place, LANES)
    lsel[...] = rem(div(place, CAP), SLOTS) * small + head * CAP + rem(place, CAP)
    wide = groups * strip

    def lane_code(i):
        lane = rem(div(i, small), SLOTS) * CAP + rem(i, CAP)
        return owner(div(i, strip)) * LANES + lane + groups * LANES * rem(div(i, CAP), size)

    sel[...] = jnp.where(lane_code(iota((wide, n), 0)) == all_rows, 1.0, 0.0).astype(jnp.bfloat16)
    back[...] = jnp.where(
        lane_code(iota((n, wide), 1)) == all_column + (groups * LANES) * div(iota((n, 1), 0), rows),
        1.0, 0.0,
    ).astype(jnp.bfloat16)
    box = (size * half, half * suf)
    for h in range(2):
        limit = spread(lengths, (size * half, rows), rem(iota((size * half, rows), 0), half) + h * half)
        kept = (div(iota(box, 1), suf) == rem(iota(box, 0), half)) & (
            rem(iota(box, 1), suf) + tp * suf < limit.astype(jnp.int32)
        )
        bias[h] = jnp.where(kept, 0.0, MASKED)

    o_copy().wait_recv()
    each(0, zs - 1, lambda i: w_copy(outward(i, zs)).start())
    each(1, zs, lambda d: a_copy(d).wait_recv())
    for d in beside:
        b_copy(d).start()

    def block_of(d):
        return rem(y - d + ys, ys)

    def c_copy(d, e):
        yy = block_of(d)
        return remote(
            xs.at[yy, e], xr.at[yy, e], c_send.at[d, e], c_recv.at[d, e], (owner(e), tp)
        )

    def c_stage(d):
        yy = block_of(d)
        for kk in range(ky):
            part = slice(kk * strip, (kk + 1) * strip)
            block = qall[pl.ds((yy * ky + kk) * dk, dk)].reshape(n, HD)
            picked = mm(sel[...], block).astype(jnp.bfloat16).reshape(groups, strip, HD)
            xs[yy, :, part, :] = picked
            xr[yy, 0, part, :] = picked[0]

    def f_copy(e, d):
        return remote(
            xr.at[y, e], xr.at[y, e], f_send.at[e - NEAR, d], f_recv.at[e - NEAR, d], y_peer(d)
        )

    def suffix(k):
        lanes = pl.ds(pl.multiple_of(k * HD, HD), HD)
        block = qall[pl.ds(k * dk, dk)].reshape(size, rows, HD)
        for h in range(2):
            part = slice(h * half, (h + 1) * half)
            at = slice(h * half * suf, (h + 1) * half * suf)
            asking = block[:, part, :].reshape(size * half, HD)
            value, level = attend(nt(asking, sk[0, at, lanes]) + bias[h], sk[1, at, lanes])
            so[k, :, part, :] = value.reshape(size, half, HD)
            sl[k, :, part, :] = jnp.broadcast_to(level, (size * half, 128)).reshape(size, half, 128)

    def suffixes(d):
        yy = block_of(d)
        for kk in range(ky):
            suffix(yy * ky + kk)

    c_stage(0)
    each(1, groups, lambda e: c_copy(0, groups - e).start())
    loads[4].wait()
    suffixes(0)

    def ask(d):
        if d == opposite:
            each(1, zs, lambda i: w_copy(i).wait_recv())
        else:
            b_copy(d).wait_recv()
        c_stage(d)
        each(1, NEAR, lambda e: c_copy(d, e).start())
        suffixes(d)

    def pass_on(e):
        c_copy(0, e).wait_recv()
        each(1, ys, lambda d: f_copy(e, d).start())

    order = [opposite] + beside
    ask(order[0])
    each(NEAR, groups, pass_on)

    loads[5].wait()

    def e_copy(d, e):
        yy = block_of(d)
        return remote(
            po.at[yy, e], pr.at[yy, e], e_send.at[d, e], e_recv.at[d, e], (asker(e), tp)
        )

    def el_copy(d, e):
        yy = block_of(d)
        return remote(
            ls.at[yy, e], lr.at[yy, e], el_send.at[d, e], el_recv.at[d, e], (asker(e), tp)
        )

    def r_copy(e, d):
        i = e - NEAR
        return remote(
            po.at[block_of(d), e], fr.at[d, i], r_send.at[i, d], r_recv.at[i, d], y_back(d)
        )

    def rl_copy(e, d):
        i = e - NEAR
        return remote(
            ls.at[block_of(d), e], flr.at[d, i], rl_send.at[i, d], rl_recv.at[i, d], y_back(d)
        )

    def m_copy(e):
        i = e - NEAR
        return remote(fo.at[i], pr.at[y, e], m_send.at[i], m_recv.at[i], (asker(e), tp))

    def ml_copy(e):
        i = e - NEAR
        return remote(fl.at[i], lr.at[y, e], ml_send.at[i], ml_recv.at[i], (asker(e), tp))

    def prefix(d):
        yy = block_of(d)
        each(1, NEAR, lambda e: c_copy(d, e).wait_recv())
        for kk in range(ky):
            lanes = pl.ds(pl.multiple_of((yy * ky + kk) * HD, HD), HD)
            for j in range(SLOTS):
                part = slice(kk * strip + j * small, kk * strip + (j + 1) * small)
                asking = xr[yy, :, part, :].reshape(groups * small, HD)
                value, level = attend(nt(asking, pk[0, j, :, lanes]), pk[1, j, :, lanes])
                value = value.astype(jnp.bfloat16).reshape(groups, small, HD)
                po[yy, :, part, :] = value
                pr[yy, 0, part, :] = value[0]
                lc[:, part, :] = jnp.broadcast_to(level, (groups * small, 128)).reshape(
                    groups, small, 128
                )

        for e in range(groups):
            ls[yy, e] = jnp.broadcast_to(to_row(lc[e], lane_rows), (8, 128))
        lr[yy, 0] = ls[yy, 0]

        def send(e):
            e_copy(d, e).start()
            el_copy(d, e).start()

        each(1, NEAR, send)

    for d in order[1:]:
        ask(d)
    prefix(0)

    def prefix_step(i):
        d = outward(i - 1, ys)
        each(NEAR, groups, lambda e: f_copy(e, d).wait_recv())
        prefix(d)

        def send(e):
            r_copy(e, d).start()
            rl_copy(e, d).start()

        each(NEAR, groups, send)

    each(1, ys, prefix_step)

    def far_merge(e):
        i = e - NEAR

        def arrived(d):
            r_copy(e, d).wait_recv()
            rl_copy(e, d).wait_recv()

        each(1, ys, arrived)
        parts = [(po[y, e].astype(jnp.float32), to_column(ls[y, e, 0:1, :], lane_rows))]
        for d in range(1, ys):
            parts.append((fr[d, i].astype(jnp.float32), to_column(flr[d, i, 0:1, :], lane_rows)))
        value, level = merge(parts)
        fo[i] = value.astype(jnp.bfloat16)
        fl[i] = jnp.broadcast_to(to_row(level, lane_rows), (8, 128))
        m_copy(e).start()
        ml_copy(e).start()

    def y_copy(d):
        return remote(yb.at[block_of(d)], yr.at[d], y_send.at[d], y_recv.at[d], y_back(d))

    def yl_copy(d):
        return remote(yl.at[block_of(d)], ylr.at[d], yl_send.at[d], yl_recv.at[d], y_back(d))

    def join(d, owners):
        yy = block_of(d)

        def arrived(e):
            e_copy(d, e).wait_recv()
            el_copy(d, e).wait_recv()

        each(1, NEAR, arrived)
        levels = jnp.full((n, 128), MASKED, jnp.float32)
        for e in range(owners):
            levels = jnp.where(gsel[...] == owner(e), lr[yy, e, 0:1, :], levels)
        for kk in range(ky):
            hit = iota((n, 128), 1) == lsel[...] + kk * strip
            level = jnp.sum(jnp.where(hit, levels, 0.0), axis=1, keepdims=True)
            parts = pr[yy, 0:owners, kk * strip : (kk + 1) * strip, :].reshape(owners * strip, HD)
            k = yy * ky + kk
            value, joint = merge(
                [
                    (mm(back[:, 0 : owners * strip], parts), level),
                    (so[k].reshape(n, HD), sl[k].reshape(n, 128)[:, 0:1]),
                ]
            )
            yb[yy, kk * dk : (kk + 1) * dk] = value.astype(jnp.bfloat16).reshape(dk, OWN * rows, HD)
            for i in range(dk // 2):
                row = to_row(joint[i * 128 : (i + 1) * 128], 128)
                yl[yy, kk * dk // 2 + i] = jnp.broadcast_to(row, (8, 128))

    across = rem(y + opposite, ys)

    def u_copy(d):
        return remote(yb.at[across, rem(z + d, zs)], ur.at[d], u_send.at[d], u_recv.at[d], z_peer(d))

    def ul_copy(d):
        return remote(
            yl.at[across, div(rem(z + d, zs), 2)], ulr.at[d], ul_send.at[d], ul_recv.at[d], z_peer(d)
        )

    def v_copy():
        return remote(vb, vr, v_send.at[0], v_recv.at[0], y_peer(opposite))

    def vl_copy():
        return remote(vl, vlr, v_send.at[1], v_recv.at[1], y_peer(opposite))

    def u_start(i):
        d = outward(i, zs)
        u_copy(d).start()
        ul_copy(d).start()

    join(opposite, NEAR)
    each(0, zs - 1, u_start)
    for d in beside:
        join(d, NEAR)
        y_copy(d).start()
        yl_copy(d).start()
    each(NEAR, groups, far_merge)

    def far_arrived(e):
        m_copy(e).wait_recv()
        ml_copy(e).wait_recv()

    each(NEAR, groups, far_arrived)
    join(0, groups)

    def u_arrived(d):
        u_copy(d).wait_recv()
        ul_copy(d).wait_recv()

    each(1, zs, u_arrived)
    shift = rem(z, 2) * 64
    parts = [(yb[across, z].astype(jnp.float32), to_column(yl[across, div(z, 2), 0:1, :], 64, shift))]
    for d in range(1, zs):
        parts.append((ur[d].astype(jnp.float32), to_column(ulr[d, 0:1, :], 64, shift)))
    value, level = merge(parts)
    vb[...] = value.astype(jnp.bfloat16)
    vl[...] = jnp.broadcast_to(to_row(level, 64), (8, 128))
    v_copy().start()
    vl_copy().start()

    def y_arrived(d):
        y_copy(d).wait_recv()
        yl_copy(d).wait_recv()

    for d in beside:
        y_arrived(d)

    def y_merge(i):
        pair = pl.ds(i * 2, 2)
        parts = [(yb[y, pair].reshape(128, HD).astype(jnp.float32), to_column(yl[y, i, 0:1, :], 128))]
        for d in beside:
            value = yr[d, pair].reshape(128, HD).astype(jnp.float32)
            parts.append((value, to_column(ylr[d, i, 0:1, :], 128)))
        value, level = merge(parts)
        zb[pair] = value.astype(jnp.bfloat16).reshape(2, 64, HD)
        zl[pair] = jnp.broadcast_to(to_row(level, 128)[None], (2, 8, 128))

    each(0, zs // 2, y_merge)

    def z_copy(d):
        return remote(zb.at[rem(z + d, zs)], zr.at[d], z_send.at[d], z_recv.at[d], z_peer(d))

    def zl_copy(d):
        return remote(zl.at[rem(z + d, zs)], zlr.at[d], zl_send.at[d], zl_recv.at[d], z_peer(d))

    def z_start(d):
        z_copy(d).start()
        zl_copy(d).start()

    each(0, zs - 1, lambda i: z_start(outward(i, zs)))

    def z_arrived(d):
        z_copy(d).wait_recv()
        zl_copy(d).wait_recv()

    each(1, zs, z_arrived)
    v_copy().wait_recv()
    vl_copy().wait_recv()
    parts = [
        (zb[z].astype(jnp.float32), to_column(zl[z, 0:1, :], 64, shift)),
        (vr[...].astype(jnp.float32), to_column(vlr[0:1, :], 64)),
    ]
    for d in range(1, zs):
        parts.append((zr[d].astype(jnp.float32), to_column(zlr[d, 0:1, :], 64, shift)))
    attended = merge(parts)[0].astype(jnp.bfloat16)
    attended = jnp.concatenate([attended[0:rows], attended[rows : 2 * rows]], axis=1)

    loads[6].wait()

    def z_order(i):
        return rem(outward(i, zs), zs)

    span = zs // 2

    def wy_copy(h, d):
        part = pl.ds(h * span, span)
        return remote(
            wp.at[block_of(d), part], wr.at[d, part], wy_send.at[h, d], wy_recv.at[h, d], y_back(d)
        )

    def wu_copy(i):
        return remote(
            wp.at[across, i], wur.at[i], wu_send.at[i], wu_recv.at[i], z_peer(z_order(i))
        )

    def wv_copy():
        return remote(wvb, wvr, wv_send.at[0], wv_recv.at[0], y_peer(opposite))

    def wz_copy(i):
        return remote(wz.at[i], wzr.at[i], wz_send.at[i], wz_recv.at[i], z_peer(z_order(i)))

    def project(h, d):
        yy = block_of(d)
        for i in range(h * span, (h + 1) * span):
            columns = (yy * zs + rem(z + z_order(i), zs)) * (OWN * HD)
            columns = pl.ds(pl.multiple_of(columns, OWN * HD), OWN * HD)
            wp[yy, i] = mm(attended, wv[:, columns]).astype(jnp.bfloat16)

    for h in range(2):
        project(h, opposite)
        each(h * span, min((h + 1) * span, zs - 1), lambda i: wu_copy(i).start())
        for d in beside:
            project(h, d)
            wy_copy(h, d).start()
    project(0, 0)
    project(1, 0)
    def y_sum(i):
        total = wp[y, i].astype(jnp.float32)
        for d in beside:
            total += wr[d, i].astype(jnp.float32)
        return total

    def w_step(i):
        wz[i] = y_sum(i).astype(jnp.bfloat16)
        wz_copy(i).start()

    def z_sent(d):
        a_copy(d).wait_send()
        z_copy(d).wait_send()
        zl_copy(d).wait_send()
        w_copy(d).wait_send()
        u_copy(d).wait_send()
        ul_copy(d).wait_send()

    each(1, zs, z_sent)

    for d in beside:
        b_copy(d).wait_send()
        y_copy(d).wait_send()
        yl_copy(d).wait_send()
    o_copy().wait_send()
    v_copy().wait_send()
    vl_copy().wait_send()

    def near_sent(d):
        def one(e):
            c_copy(d, e).wait_send()
            e_copy(d, e).wait_send()
            el_copy(d, e).wait_send()

        each(1, NEAR, one)

    def far_sent(e):
        def one(d):
            f_copy(e, d).wait_send()
            r_copy(e, d).wait_send()
            rl_copy(e, d).wait_send()

        c_copy(0, e).wait_send()
        each(1, ys, one)
        m_copy(e).wait_send()
        ml_copy(e).wait_send()

    each(0, ys, near_sent)
    each(NEAR, groups, far_sent)

    for d in beside:
        wy_copy(0, d).wait_recv()
    each(0, span, w_step)
    each(0, zs - 1, lambda i: wu_copy(i).wait_recv())
    total = wp[across, zs - 1].astype(jnp.float32)
    for i in range(zs - 1):
        total += wur[i].astype(jnp.float32)
    wvb[...] = total.astype(jnp.bfloat16)
    wv_copy().start()
    for d in beside:
        wy_copy(1, d).wait_recv()
    each(span, zs - 1, w_step)
    total = y_sum(zs - 1)
    wv_copy().wait_recv()
    total += wvr[...].astype(jnp.float32)
    each(0, zs - 1, lambda i: wz_copy(i).wait_recv())
    for i in range(zs - 1):
        total += wzr[i].astype(jnp.float32)
    out_ref[...] = total.astype(jnp.bfloat16)

    def last_sent(i):
        wu_copy(i).wait_send()
        wz_copy(i).wait_send()

    each(0, zs - 1, last_sent)
    for d in beside:
        wy_copy(0, d).wait_send()
        wy_copy(1, d).wait_send()
    wv_copy().wait_send()


def body(zs, queries, prefix_ids, suffix_lengths, owner_slots, prefix_cache, suffix_cache, wo):
    groups = lax.axis_size("grp")
    shards = lax.axis_size("tp")
    ys = shards // zs
    rows = queries.shape[0]
    suf = suffix_cache.shape[2]
    kvh = prefix_cache.shape[3] // HD
    size = shards * OWN // kvh
    n = size * rows
    ky = kvh // ys
    strip = SLOTS * size * CAP
    lane_rows = ky * strip
    far = groups - NEAR

    dims = (groups, ys, zs, kvh, rows, suf)
    bf, f32 = jnp.bfloat16, jnp.float32
    dma = pltpu.SemaphoreType.DMA
    vmem = pl.BlockSpec(memory_space=pltpu.VMEM)
    hbm = pl.BlockSpec(memory_space=pltpu.HBM)
    V = pltpu.VMEM
    scratch = [
        V(queries.shape, bf),
        V((1, rows), jnp.int32),
        V((1, rows), jnp.int32),
        V((1, owner_slots.shape[0]), jnp.int32),
        V(prefix_cache.shape, bf),
        V((2, rows * suf, kvh * HD), bf),
        V(wo.shape, bf),
        V((shards, OWN * rows, HD), bf),
        V((ys, groups, lane_rows, HD), bf),
        V((ys, groups, lane_rows, HD), bf),
        V((ys, groups, lane_rows, HD), bf),
        V((ys, groups, lane_rows, HD), bf),
        V((ys, groups, 8, 128), f32),
        V((ys, groups, 8, 128), f32),
        V((ys, far, lane_rows, HD), bf),
        V((ys, far, 8, 128), f32),
        V((far, lane_rows, HD), bf),
        V((far, 8, 128), f32),
        V((groups, lane_rows, 128), f32),
        V((kvh, size, rows, HD), f32),
        V((kvh, size, rows, 128), f32),
        V((groups * strip, n), bf),
        V((n, groups * strip), bf),
        V((n, 128), jnp.int32),
        V((n, 128), jnp.int32),
        V((2, n // 2, rows * suf // 2), f32),
        V((ys, zs, OWN * rows, HD), bf),
        V((ys, zs // 2, 8, 128), f32),
        V((ys, zs, OWN * rows, HD), bf),
        V((ys, zs // 2, 8, 128), f32),
        V((zs, OWN * rows, HD), bf),
        V((zs, 8, 128), f32),
        V((OWN * rows, HD), bf),
        V((8, 128), f32),
        V((OWN * rows, HD), bf),
        V((8, 128), f32),
        V((zs, OWN * rows, HD), bf),
        V((zs, 8, 128), f32),
        V((zs, OWN * rows, HD), bf),
        V((zs, 8, 128), f32),
        V((ys, zs, rows, OWN * HD), bf),
        V((ys, zs, rows, OWN * HD), bf),
        V((zs, rows, OWN * HD), bf),
        V((zs, rows, OWN * HD), bf),
        V((zs, rows, OWN * HD), bf),
        V((rows, OWN * HD), bf),
        V((rows, OWN * HD), bf),
        dma((7,)),
        dma((zs,)), dma((zs,)),
        dma((ys,)), dma((ys,)),
        dma((1,)), dma((1,)),
        dma((zs,)), dma((zs,)),
        dma((ys, groups)), dma((ys, groups)),
        dma((far, ys)), dma((far, ys)),
        dma((ys, groups)), dma((ys, groups)),
        dma((ys, groups)), dma((ys, groups)),
        dma((far, ys)), dma((far, ys)),
        dma((far, ys)), dma((far, ys)),
        dma((far,)), dma((far,)),
        dma((far,)), dma((far,)),
        dma((ys,)), dma((ys,)), dma((ys,)), dma((ys,)),
        dma((zs,)), dma((zs,)), dma((zs,)), dma((zs,)),
        dma((zs,)), dma((zs,)), dma((zs,)), dma((zs,)),
        dma((2,)), dma((2,)),
        dma((zs,)), dma((zs,)),
        dma((1,)), dma((1,)),
        dma((2, ys)), dma((2, ys)),
        dma((zs,)), dma((zs,)),
    ]
    return pl.pallas_call(
        functools.partial(kernel, dims),
        out_shape=jax.ShapeDtypeStruct((rows, wo.shape[1] // shards), bf),
        in_specs=[hbm] * 7,
        out_specs=vmem,
        scratch_shapes=scratch,
        compiler_params=pltpu.CompilerParams(
            collective_id=0, has_side_effects=True, vmem_limit_bytes=62 * 1024 * 1024
        ),
        name="decode_attention",
    )(
        queries, prefix_ids.reshape(1, rows), suffix_lengths.reshape(1, rows),
        owner_slots.reshape(1, -1), prefix_cache,
        suffix_cache.reshape(2, rows * suf, kvh * HD), wo,
    )


def solution(mesh, zs=Z_SIZE):
    placed = (
        P("grp", "tp"),
        P("grp", None),
        P("grp"),
        P(),
        P(None, "grp", "tp", None),
        P(None, "grp", "tp", None),
        P("tp", None),
    )
    return jax.shard_map(
        functools.partial(body, zs),
        mesh=mesh, in_specs=placed, out_specs=P("grp", "tp"), check_vma=False,
    )
```

profile of v0, /device:TPU:2, one launch (start us, length us, event | category | flops | bytes accessed | tf_op | source)
XLA Modules:
  0.0 59.4 jit_solution(17354252745971183624)
XLA Ops:
  0.0 58.0 %decode_attention.1 = bf16[32,256]{1,0:T(8,128)(2,1)} custom-call(bf16[32,256]{1,0:T(8,128)(2,1)} %q_ref.1, s32[1,32]{1,0:T(1,128)} %bitcast.5, s32[1,32]{1,0:T(1,128)} %bitcast.6, s32[1,16]{1,0:T(1,128)} %bitcast.7, bf16[2,2,256,1024]{3,2,1,0:T(8,128)(2,1)} %pc_ref.1, bf16[2,512,1024]{2,1,0:T(8,128)(2,1)} %bitcast.4, bf16[256,8192]{1,0:T(8,128)(2,1)} %wo_ref.1), custom_call_target="tpu_custom_call" | custom-call | tf_op jit(solution)/shard_map/decode_attention/pallas_call | solution.py:726
  58.0 1.3 %copy.9 = bf16[32,256]{1,0:T(8,128)(2,1)} copy(bf16[32,256]{1,0:T(8,128)(2,1)} %decode_attention.1) | data formatting | bytes 32768
where the time goes:
time: 59.6 us; the launch traced here: 59.4 us
  Pallas kernels  58 us (97%)
  local copies, waits for them, and re-layouts  1.32 us (2%)
    pallas_call x1, Pallas kernels, body(): pl.pallas_call(functools.partial(kernel, dims), out_shape=jax.ShapeDtypeS...  58 us
    unnamed x1, local copies, waits for them, and re-layouts  1.32 us

commit v1 on v0

--- a/solution.py
+++ b/solution.py
@@ -339,7 +339,7 @@
                 )
 
         for e in range(groups):
-            ls[yy, e] = jnp.broadcast_to(to_row(lc[e], lane_rows), (8, 128))
+            ls[yy, e] = to_row(lc[e], lane_rows)
         lr[yy, 0] = ls[yy, 0]
 
         def send(e):
@@ -378,7 +378,7 @@
             parts.append((fr[d, i].astype(jnp.float32), to_column(flr[d, i, 0:1, :], lane_rows)))
         value, level = merge(parts)
         fo[i] = value.astype(jnp.bfloat16)
-        fl[i] = jnp.broadcast_to(to_row(level, lane_rows), (8, 128))
+        fl[i] = to_row(level, lane_rows)
         m_copy(e).start()
         ml_copy(e).start()
 
@@ -413,7 +413,7 @@
             yb[yy, kk * dk : (kk + 1) * dk] = value.astype(jnp.bfloat16).reshape(dk, OWN * rows, HD)
             for i in range(dk // 2):
                 row = to_row(joint[i * 128 : (i + 1) * 128], 128)
-                yl[yy, kk * dk // 2 + i] = jnp.broadcast_to(row, (8, 128))
+                yl[yy, kk * dk // 2 + i] = row
 
     across = rem(y + opposite, ys)
 
@@ -462,7 +462,7 @@
         parts.append((ur[d].astype(jnp.float32), to_column(ulr[d, 0:1, :], 64, shift)))
     value, level = merge(parts)
     vb[...] = value.astype(jnp.bfloat16)
-    vl[...] = jnp.broadcast_to(to_row(level, 64), (8, 128))
+    vl[...] = to_row(level, 64)
     v_copy().start()
     vl_copy().start()
 
@@ -481,7 +481,7 @@
             parts.append((value, to_column(ylr[d, i, 0:1, :], 128)))
         value, level = merge(parts)
         zb[pair] = value.astype(jnp.bfloat16).reshape(2, 64, HD)
-        zl[pair] = jnp.broadcast_to(to_row(level, 128)[None], (2, 8, 128))
+        zl[pair] = jnp.broadcast_to(to_row(level, 128)[None], (2, 1, 128))
 
     each(0, zs // 2, y_merge)
 
@@ -666,12 +666,12 @@
         V((ys, groups, lane_rows, HD), bf),
         V((ys, groups, lane_rows, HD), bf),
         V((ys, groups, lane_rows, HD), bf),
-        V((ys, groups, 8, 128), f32),
-        V((ys, groups, 8, 128), f32),
+        V((ys, groups, 1, 128), f32),
+        V((ys, groups, 1, 128), f32),
         V((ys, far, lane_rows, HD), bf),
-        V((ys, far, 8, 128), f32),
+        V((ys, far, 1, 128), f32),
         V((far, lane_rows, HD), bf),
-        V((far, 8, 128), f32),
+        V((far, 1, 128), f32),
         V((groups, lane_rows, 128), f32),
         V((kvh, size, rows, HD), f32),
         V((kvh, size, rows, 128), f32),
@@ -681,19 +681,19 @@
         V((n, 128), jnp.int32),
         V((2, n // 2, rows * suf // 2), f32),
         V((ys, zs, OWN * rows, HD), bf),
-        V((ys, zs // 2, 8, 128), f32),
+        V((ys, zs // 2, 1, 128), f32),
         V((ys, zs, OWN * rows, HD), bf),
-        V((ys, zs // 2, 8, 128), f32),
+        V((ys, zs // 2, 1, 128), f32),
         V((zs, OWN * rows, HD), bf),
-        V((zs, 8, 128), f32),
+        V((zs, 1, 128), f32),
         V((OWN * rows, HD), bf),
-        V((8, 128), f32),
+        V((1, 128), f32),
         V((OWN * rows, HD), bf),
-        V((8, 128), f32),
+        V((1, 128), f32),
         V((zs, OWN * rows, HD), bf),
-        V((zs, 8, 128), f32),
+        V((zs, 1, 128), f32),
         V((zs, OWN * rows, HD), bf),
-        V((zs, 8, 128), f32),
+        V((zs, 1, 128), f32),
         V((ys, zs, rows, OWN * HD), bf),
         V((ys, zs, rows, OWN * HD), bf),
         V((zs, rows, OWN * HD), bf),

time: 59.6 us -> 58.7 us (0.985)
  Pallas kernels: 58 us -> 57.1 us
    pallas_call x1, Pallas kernels: 58 us -> 57.1 us  [body(): pl.pallas_call(functools.partial(kernel, dims), out_shape=jax.ShapeDtypeS...]
where the time goes in v1:
time: 58.7 us; the launch traced here: 58.4 us
  Pallas kernels  57.1 us (97%)
  local copies, waits for them, and re-layouts  1.32 us (2%)
    pallas_call x1, Pallas kernels, body(): pl.pallas_call(functools.partial(kernel, dims), out_shape=jax.ShapeDtypeS...  57.1 us
    unnamed x1, local copies, waits for them, and re-layouts  1.32 us

profile of v1, /device:TPU:2, one launch (start us, length us, event | category | flops | bytes accessed | tf_op | source)
XLA Modules:
  0.0 58.4 jit_solution(6945968124102903722)
XLA Ops:
  0.0 57.1 %decode_attention.1 = bf16[32,256]{1,0:T(8,128)(2,1)} custom-call(bf16[32,256]{1,0:T(8,128)(2,1)} %q_ref.1, s32[1,32]{1,0:T(1,128)} %bitcast.5, s32[1,32]{1,0:T(1,128)} %bitcast.6, s32[1,16]{1,0:T(1,128)} %bitcast.7, bf16[2,2,256,1024]{3,2,1,0:T(8,128)(2,1)} %pc_ref.1, bf16[2,512,1024]{2,1,0:T(8,128)(2,1)} %bitcast.4, bf16[256,8192]{1,0:T(8,128)(2,1)} %wo_ref.1), custom_call_target="tpu_custom_call" | custom-call | tf_op jit(solution)/shard_map/decode_attention/pallas_call | solution.py:726
  57.1 1.3 %copy.9 = bf16[32,256]{1,0:T(8,128)(2,1)} copy(bf16[32,256]{1,0:T(8,128)(2,1)} %decode_attention.1) | data formatting | bytes 32768
